TPU v7x, 1024 devices: a whole 8x8x8 slice. The times are simulated.
1024 devices in a mesh: pipe: 16 (over x, y_hi), expert: 64 (over y_lo, z, core).
Axes of the slice: x: 8, y: 8 (y_hi: 2, y_lo: 4; y = y_hi * 4 + y_lo), z: 8, core: 2. Of those that a mesh axis runs over, the one named last changes fastest.
Arguments:
- hidden_a: bfloat16 [64, 768, 2048], P('expert'), may hold values from -6 to 6
- expert_weights: bfloat16 [64, 2048, 7168], P('expert', None, 'pipe'), may hold values from -0.125 to 0.125
- routes_a: int32 [4096, 8], P('expert'), may hold values from 0 to 63, all different within a row; in each aligned block of 64 rows (0 to 63, 64 to 127, ...) at most 12 rows name the same one
- gates_a: float32 [4096, 8], P('expert'), may hold values from 0.05 to 0.6
- cotangent_b: bfloat16 [4096, 7168], P('expert', 'pipe'), may hold values from -6 to 6
- routes_b: int32 [4096, 8], P('expert'), may hold values from 0 to 63, all different within a row; in each aligned block of 64 rows (0 to 63, 64 to 127, ...) at most 12 rows name the same one
- gates_b: float32 [4096, 8], P('expert'), may hold values from 0.05 to 0.6
Outputs:
- mixed_a: bfloat16 [4096, 7168], P('expert', 'pipe')
- grad_hidden_b: bfloat16 [64, 768, 2048], P('expert', None, 'pipe')
Inputs may be any that keep to these rules, and one draw needn't show every extreme that they name: `routes_a`: among the tokens of one index of expert (aligned blocks of 64 rows), no expert is chosen more than 12 times, a bound that some block reaches; the 8 experts of a token differ. `routes_b`: among the tokens of one index of expert (aligned blocks of 64 rows), no expert is chosen more than 12 times, a bound that some block reaches; the 8 experts of a token differ.
All inputs are finite; a program needn't handle non-finite values.
Results may differ from a plain program's by a relative error of at most 0.019.
Values may be sent and summed in bfloat16 or wider, within the bound.
A program may use at most 64 MiB of HBM per device.

v0:
```python
import jax
import jax.numpy as jnp
from jax import lax
from jax.sharding import PartitionSpec as P


def local_slots(routes, total):
    flat = routes.reshape(-1)
    onehot = (flat[:, None] == jnp.arange(total, dtype=jnp.int32)[None, :]).astype(jnp.int32)
    ranks = jnp.cumsum(onehot, axis=0) - onehot
    return jnp.sum(ranks * onehot, axis=1).reshape(routes.shape)


def on_device(hidden_a, expert_weights, routes_a, gates_a, cotangent_b, routes_b, gates_b):
    groups = lax.axis_size("expert")
    local = expert_weights.shape[0]
    total = local * groups
    cap = hidden_a.shape[1] // groups
    width = cotangent_b.shape[1]
    outputs = jnp.einsum(
        "erf,efd->erd", hidden_a, expert_weights, preferred_element_type=jnp.float32
    )
    flat = lax.all_to_all(
        outputs.astype(jnp.bfloat16).reshape(local, groups, cap, width),
        "expert",
        split_axis=1,
        concat_axis=0,
        tiled=True,
    ).reshape(total * cap, width)
    index = routes_a * cap + local_slots(routes_a, total)
    picked = flat[index]
    mixed = jnp.einsum("tk,tkd->td", gates_a, picked.astype(jnp.float32))
    mixed_a = mixed.astype(jnp.bfloat16)
    slots = local_slots(routes_b, total)
    index = routes_b % local * (groups * cap) + routes_b // local * cap + slots
    values = (gates_b[:, :, None] * cotangent_b[:, None, :].astype(jnp.float32)).astype(
        jnp.bfloat16
    )
    buffer = jnp.zeros((local * groups * cap, width), jnp.bfloat16)
    buffer = buffer.at[index.reshape(-1)].set(values.reshape(-1, width))
    arrived = lax.all_to_all(
        buffer.reshape(local, groups, cap, width), "expert", split_axis=1, concat_axis=0, tiled=True
    )
    partial_value = jnp.einsum(
        "secd,efd->escf", arrived, expert_weights, preferred_element_type=jnp.float32
    )
    summed = lax.psum_scatter(
        partial_value.astype(jnp.bfloat16), "pipe", scatter_dimension=3, tiled=True
    ).astype(jnp.float32)
    grad_hidden_b = summed.reshape(local, groups * cap, summed.shape[3]).astype(jnp.bfloat16)
    return (mixed_a, grad_hidden_b)


def solution(mesh):
    in_specs = (
        P("expert", None, None),
        P("expert", None, "pipe"),
        P("expert", None),
        P("expert", None),
        P("expert", "pipe"),
        P("expert", None),
        P("expert", None),
    )
    out_specs = (P("expert", "pipe"), P("expert", None, "pipe"))
    return jax.shard_map(
        on_device, mesh=mesh, in_specs=in_specs, out_specs=out_specs, check_vma=False
    )
```

profile of v0, /device:TPU:1, one launch (start us, length us, event | category | flops | bytes accessed | tf_op | source)
XLA Modules:
  0.0 343.6 jit_solution(13943124036276494842)
XLA Ops:
  7.2 0.0 copy-start
  7.2 0.0 reduce-scatter.4.cloned.1.call-start
  7.2 0.9 copy.47
  8.1 0.1 eq.64
  8.2 0.1 eq.60
  8.3 1.2 reduce-window.16
  9.6 0.2 slice_reduce_fusion
  9.8 0.1 fusion.22
  10.0 0.1 reshape.135
  10.1 0.1 copy.50
  10.1 0.7 multiply_add_fusion
  10.8 0.1 copy.51
  10.9 0.1 reshape.136
  11.0 0.9 convert_element_type.55
  11.9 0.8 copy.52
  12.6 0.1 mul.35
  12.7 3.4 scatter_custom_fusion
  16.2 2.3 reshape.137
  18.4 50.7 %all_to_all.8 = bf16[1,64,12,448]{3,2,0,1:T(8,128)(2,1)S(1)} all-to-all(bf16[1,64,12,448]{3,2,0,1:T(8,128)(2,1)} %bitcast.79), channel_id=1, replica_groups=mesh['pipe'=16,'expert'=64] {'expert'}, dimensions={1} | all-to-all | bytes 1376256 | tf_op jit(solution)/shard_map/all_to_all | solution.py:41
  69.2 5.2 %fusion.2 = bf16[1,64,12,2048]{3,1,2,0:T(8,128)(2,1)} fusion(bf16[1,2048,448]{1,2,0:T(8,128)(2,1)} %param.8, bf16[1,64,12,448]{3,2,0,1:T(8,128)(2,1)S(1)} %all_to_all.8), kind=kOutput, calls=%fused_computation.5 | convolution fusion | flops 1410859008 | bytes 5668864 | tf_op jit(solution)/shard_map/secd,efd->escf/dot_general | solution.py:44
  74.4 10.5 %copy.58 = bf16[1,64,12,2048]{1,2,0,3:T(8,128)(2,1)} copy(bf16[1,64,12,2048]{3,1,2,0:T(8,128)(2,1)} %fusion.2) | data formatting | bytes 6291456
  84.9 11.1 %reshape.160 = bf16[2048,768]{1,0:T(8,128)(2,1)} reshape(bf16[2048,1,12,64]{3,2,1,0:T(8,128)(2,1)} %bitcast.77) | data formatting | bytes 6291456
  96.0 0.0 reduce-scatter.4.cloned.1.call-update
  96.0 0.0 copy-done
  96.0 4.0 %fusion.5 = bf16[768,448]{0,1:T(8,128)(2,1)} fusion(bf16[1,2048,448]{1,2,0:T(8,128)(2,1)} %param.8, bf16[1,768,2048]{2,1,0:T(8,128)(2,1)S(1)} %copy-done), kind=kOutput, calls=%fused_computation.8 | convolution fusion | flops 1409630208 | bytes 5668864 | tf_op jit(solution)/shard_map/erf,efd->erd/dot_general | solution.py:20
  100.0 0.0 copy-start.1
  100.0 0.0 copy-start.2
  100.0 2.3 copy.40
  102.3 2.3 reshape.130
  104.6 6.1 %all-to-all-start = ((bf16[1,64,12,448]{3,2,0,1:T(8,128)(2,1)}), bf16[1,64,12,448]{3,2,0,1:T(8,128)(2,1)}, u32[]{:S(2)}, u32[]{:S(2)}) async-start(bf16[1,64,12,448]{3,2,0,1:T(8,128)(2,1)} %bitcast.78), calls=%async_computation | async-start | bytes 2097152 | tf_op jit(solution)/shard_map/all_to_all | solution.py:23
  110.8 0.0 copy-done.1
  110.8 0.1 copy.42
  110.9 0.1 eq.56
  111.0 0.1 eq.52
  111.1 1.2 reduce-window.14
  112.3 0.2 slice_reduce_fusion.1
  112.6 0.1 fusion.25
  112.7 0.1 reshape.133
  112.8 0.1 copy.45
  112.8 0.1 copy.46
  112.9 0.1 reshape.141
  113.0 0.0 copy-done.2
  113.0 0.1 copy.56
  113.2 29.7 %all-to-all-done = bf16[1,64,12,448]{3,2,0,1:T(8,128)(2,1)} async-done(((bf16[1,64,12,448]{3,2,0,1:T(8,128)(2,1)}), bf16[1,64,12,448]{3,2,0,1:T(8,128)(2,1)}, u32[]{:S(2)}, u32[]{:S(2)}) %all-to-all-start) | async-done | bytes 688160 | tf_op jit(solution)/shard_map/all_to_all | solution.py:23
  142.9 2.3 reshape.131
  145.1 3.9 %gather_fusion = bf16[512,448]{1,0:T(8,128)(2,1)} fusion(bf16[768,448]{1,0:T(8,128)(2,1)} %reshape.131, s32[1024]{0:T(1024)S(1)} %pad_clamp_fusion), kind=kCustom, calls=%fused_computation | custom fusion | bytes 919552 | tf_op jit(solution)/shard_map/gather | solution.py:31
  149.0 1.3 fusion.15
  150.3 0.6 copy.70
  151.0 181.4 %reduce-scatter.4.cloned.1.call-done = bf16[128,768]{1,0:T(8,128)(2,1)} async-done(((bf16[2048,768]{1,0:T(8,128)(2,1)}), bf16[128,768]{1,0:T(8,128)(2,1)}) %reduce-scatter.4.cloned.1.call-update) | async-done | bytes 196624
  332.4 2.1 reshape.161
  334.4 1.6 copy.55
  336.0 0.7 convert_element_type.59
  (9 shorter events, 0.1 us)
Async XLA Ops:
  7.2 88.9 %copy-start = (bf16[1,768,2048]{2,1,0:T(8,128)(2,1)S(1)}, bf16[1,768,2048]{2,1,0:T(8,128)(2,1)}, u32[]{:S(2)}) copy-start(bf16[1,768,2048]{2,1,0:T(8,128)(2,1)} %param.7) | copy-start | bytes 9437188
  7.2 325.2 %reduce-scatter.4.cloned.1.call-start = ((), (), s32[]{:S(2)}) async-start(), calls=%async_computation.3 | async-start | bytes 3342336
  100.0 10.8 %copy-start.1 = (s32[64,8]{0,1:T(8,128)S(1)}, s32[64,8]{0,1:T(8,128)}, u32[]{:S(2)}) copy-start(s32[64,8]{0,1:T(8,128)} %param.9) | copy-start | bytes 6148
  100.0 13.0 %copy-start.2 = (f32[64,8]{0,1:T(8,128)S(1)}, f32[64,8]{0,1:T(8,128)}, u32[]{:S(2)}) copy-start(f32[64,8]{0,1:T(8,128)} %param.10) | copy-start | bytes 6148
  104.6 38.2 %all-to-all-start = ((bf16[1,64,12,448]{3,2,0,1:T(8,128)(2,1)}), bf16[1,64,12,448]{3,2,0,1:T(8,128)(2,1)}, u32[]{:S(2)}, u32[]{:S(2)}) async-start(bf16[1,64,12,448]{3,2,0,1:T(8,128)(2,1)} %bitcast.78), calls=%async_computation | async-start | bytes 2097152 | tf_op jit(solution)/shard_map/all_to_all | solution.py:23
Sparse Core Ops, SparseCore 0:
  96.1 236.1 reduce-scatter.3
where the time goes:
time: 349 us; the launch traced here: 344 us
  waiting for transfers between devices  211 us (60%)
  blocking collectives  50.7 us (15%)
  local copies, waits for them, and re-layouts  43.1 us (12%)
  between operations  14.2 us (4%)
  matrix products  10.5 us (3%)
  other arithmetic  7.76 us (2%)
  starting transfers between devices  6.18 us (2%)
    unnamed x2, waiting for transfers between devices  181 us
    all_to_all x1, blocking collectives, on_device(): lax.all_to_all(buffer.reshape(local, groups, cap, width), 'expert', split...  50.7 us
    all_to_all x1, waiting for transfers between devices, on_device(): lax.all_to_all(outputs.astype(jnp.bfloat16).reshape(local, groups, cap, w...  29.7 us
    unnamed x13, local copies, waits for them, and re-layouts  25.5 us
  transfers between devices with their start and end apart: 2, of which 2 were waited for; matrix products, arithmetic and copies ran while one was open for 6% of the time, Pallas kernels for 0%

commit v1 on v0

v1 whole, which is shorter than its diff:
```python
import functools

import jax
import jax.numpy as jnp
from jax import lax
from jax.experimental import pallas as pl
from jax.experimental.pallas import tpu as pltpu
from jax.sharding import PartitionSpec as P

NX, NYH = 8, 2
NY, NZ, NC = 4, 8, 2
SEND_A, COMBINE_A = 1, 9

BF16, F32 = jnp.bfloat16, jnp.float32


def body(
    cap,
    h_hbm, w_hbm, ra_ref, ga_ref, cot_ref, rb_ref, gb_ref,
    mixed_ref, grad_ref,
    h_vm, w_vm, gath, codes, fwd, tile48, asend, arecv, bsend, brecv, pa,
    pbuf, splus, sminus, rplus, rminus, fin, hsend, hrecv, out4, gout,
    dense, dsend, drecv,
    load_sem, y_s, y_r, az_s, az_r, bz_s, bz_r, xp_s, xp_r, xm_s, xm_r,
    h_s, h_r, d_s, d_r,
):
    tok, width = cot_ref.shape
    top = ra_ref.shape[1]
    total = NY * NZ * NC
    msg = NY * cap
    half = NX // 2
    wide = gath.shape[2]
    p = lax.axis_index("pipe")
    e = lax.axis_index("expert")
    x, yh = p // NYH, p % NYH
    y, z, c = e // (NZ * NC), (e // NC) % NZ, e % NC

    def dev(x=x, yh=yh, y=y, z=z, c=c):
        return {"pipe": x * NYH + yh, "expert": (y * NZ + z) * NC + c}

    def z_step(k):
        if isinstance(k, int):
            return (k + 1) // 2 if k % 2 else (NZ - k // 2) % NZ
        return lax.select(k % 2 == 1, (k + 1) // 2, (NZ - k // 2) % NZ)

    def remote(src, dst, send, recv, to):
        return pltpu.make_async_remote_copy(
            src_ref=src, dst_ref=dst, send_sem=send, recv_sem=recv,
            device_id=to, device_id_type=pl.DeviceIdType.MESH,
        )

    load_w = pltpu.make_async_copy(w_hbm, w_vm, load_sem.at[0])
    load_h = pltpu.make_async_copy(h_hbm, h_vm, load_sem.at[1])
    load_w.start()
    load_h.start()

    partners = [dev(y=(y + d) % NY) for d in range(1, NY)]
    partners += [
        dev(z=(z + d) % NZ, c=(c + f) % NC)
        for d in range(NZ) for f in range(NC) if d or f
    ]
    partners += [dev(x=(x + 1) % NX), dev(x=(x + NX - 1) % NX), dev(yh=1 - yh)]
    barrier = pltpu.get_barrier_semaphore()
    for to in partners:
        pl.semaphore_signal(
            barrier, inc=1, device_id=to, device_id_type=pl.DeviceIdType.MESH
        )

    lane = lax.broadcasted_iota(jnp.int32, (tok, 128), 1)
    base = width - (wide - 128)
    tail = jnp.dot(
        cot_ref[:, wide - 128:],
        (
            lax.broadcasted_iota(jnp.int32, (base, 128), 0)
            == lax.broadcasted_iota(jnp.int32, (base, 128), 1)
        ).astype(F32).astype(BF16),
        preferred_element_type=F32,
    )
    before = (
        lax.broadcasted_iota(jnp.int32, (tok, tok), 0)
        > lax.broadcasted_iota(jnp.int32, (tok, tok), 1)
    ).astype(F32).astype(BF16)
    for n, (r_ref, g_ref) in enumerate(((ra_ref, ga_ref), (rb_ref, gb_ref))):
        first = base + n * 4 * 8
        routes = r_ref[...]
        gates = g_ref[...]
        high = gates.astype(BF16).astype(F32)
        low = (gates - high).astype(BF16).astype(F32)
        names = routes.astype(F32)
        hit = [routes[:, k:k + 1] == lane for k in range(top)]
        member = jnp.zeros((tok, 128), F32)
        for k in range(top):
            member = jnp.where(hit[k], 1.0, member)
        rank = jnp.dot(before, member.astype(BF16), preferred_element_type=F32)
        for k in range(top):
            slot = jnp.sum(jnp.where(hit[k], rank, 0.0), axis=1, keepdims=True)
            tail = jnp.where(lane == first + k, names[:, k:k + 1], tail)
            tail = jnp.where(lane == first + 8 + k, slot, tail)
            tail = jnp.where(lane == first + 16 + k, high[:, k:k + 1], tail)
            tail = jnp.where(lane == first + 24 + k, low[:, k:k + 1], tail)
    gath[0, :, :wide - 128] = cot_ref[:, :wide - 128]
    gath[0, :, wide - 128:] = tail.astype(BF16)

    pl.semaphore_wait(barrier, len(partners))

    def y_copy(d):
        return remote(
            gath.at[0], gath.at[d], y_s.at[d - 1], y_r.at[d - 1],
            dev(y=(y + d) % NY),
        )

    for d in (2, 1, 3):
        if d < NY:
            y_copy(d).start()

    load_w.wait()
    load_h.wait()
    rows = NZ * NC * cap

    def forward(j, carry):
        value = jnp.dot(
            h_vm[pl.ds(pl.multiple_of(j * rows, 16), rows), :], w_vm[...],
            preferred_element_type=F32,
        )
        for i in range(NZ * NC):
            fwd[j * (NZ * NC) + i, 0:cap, :] = value[i * cap:(i + 1) * cap, :]
        return carry

    lax.fori_loop(0, NY, forward, 0)

    def pack_a(k, carry):
        to = ((z + z_step(k)) % NZ) * NC
        for f in range(NC):
            for r in range(NY):
                source = ((y + NY - r) % NY) * (NZ * NC) + to + (c + f) % NC
                tile48[r * cap:(r + 1) * cap, :] = fwd[source, 0:cap, :]
            asend[k * NC + f] = tile48[...].astype(BF16)
        return carry

    lax.fori_loop(0, NZ, pack_a, 0)
    arecv[0] = asend[0]

    for d in range(1, NY):
        y_copy(d).wait_recv()

    for n in range(2):
        for r in range(NY):
            info = gath[r, :, wide - 128:].astype(F32).T
            first = base + n * 4 * 8
            cols = slice(r * tok, (r + 1) * tok)
            codes[n, 0, :, cols] = (
                info[first:first + 8] * 16.0 + info[first + 8:first + 16]
            )
            codes[n, 1, :, cols] = info[first + 16:first + 24]
            codes[n, 2, :, cols] = info[first + 24:first + 32]

    row = lax.broadcasted_iota(jnp.int32, (msg, NY * tok), 0)
    col = lax.broadcasted_iota(jnp.int32, (msg, NY * tok), 1)
    slot_code = jnp.full((msg, NY * tok), -4096.0, F32)
    for r in range(NY):
        inside = (
            (row >= r * cap) & (row < (r + 1) * cap)
            & (col >= r * tok) & (col < (r + 1) * tok)
        )
        slot_code = jnp.where(inside, (row - r * cap).astype(F32), slot_code)

    def pairs(n, expert):
        want = slot_code + (expert * 16).astype(F32)
        high = jnp.zeros((msg, NY * tok), F32)
        low = jnp.zeros((msg, NY * tok), F32)
        for k in range(top):
            same = want == codes[n, 0, k:k + 1, :]
            high = jnp.where(same, codes[n, 1, k:k + 1, :], high)
            low = jnp.where(same, codes[n, 2, k:k + 1, :], low)
        return high.astype(BF16), low.astype(BF16)

    def bz_copy(k, f):
        m = k * NC + f
        return remote(
            bsend.at[m], brecv.at[m], bz_s.at[m], bz_r.at[m],
            dev(z=(z + z_step(k)) % NZ, c=(c + f) % NC),
        )

    def az_copy(k, f):
        m = k * NC + f
        return remote(
            asend.at[m], arecv.at[m], az_s.at[m], az_r.at[m],
            dev(z=(z + z_step(k)) % NZ, c=(c + f) % NC),
        )

    def fill(k, f):
        expert = (y * NZ + (z + z_step(k)) % NZ) * NC + (c + f) % NC
        high, low = pairs(1, expert)
        cots = gath[...].reshape(NY * tok, wide)
        value = jnp.dot(high, cots, preferred_element_type=F32)
        value += jnp.dot(low, cots, preferred_element_type=F32)
        return value[:, :width].astype(BF16)

    for f in range(1, NC):
        bsend[f] = fill(0, f)
        bz_copy(0, f).start()

    def fill_step(k, carry):
        for f in range(NC):
            bsend[k * NC + f] = fill(k, f)
            bz_copy(k, f).start()
        return carry

    lax.fori_loop(1, NZ, fill_step, 0)
    brecv[0] = fill(0, 0)

    block = NC * msg

    def plus(k, s):
        to, sems = dev(x=(x + 1) % NX), (xp_s.at[k, s], xp_r.at[k, s])
        if s == 0:
            return remote(splus.at[k, s, 0], rplus.at[k, s, 0], *sems, to)
        return remote(splus.at[k, s], rplus.at[k, s], *sems, to)

    def minus(k, s):
        to, sems = dev(x=(x + NX - 1) % NX), (xm_s.at[k, s], xm_r.at[k, s])
        if s == 0:
            return remote(sminus.at[k, s, 1], rminus.at[k, s, 1], *sems, to)
        return remote(sminus.at[k, s], rminus.at[k, s], *sems, to)

    def swap(k):
        return remote(
            hsend.at[k], hrecv.at[k], h_s.at[k], h_r.at[k], dev(yh=1 - yh)
        )

    def product(k):
        @pl.when(k > 0)
        def _():
            bz_copy(k, 0).wait_recv()

        for f in range(1, NC):
            bz_copy(k, f).wait_recv()
        value = brecv[pl.ds(k * NC, NC)].reshape(block, width)
        order = [half]
        for i in range(half - 1, 0, -1):
            order += [i, NX - i]
        for off in order + [0]:
            q = (x + off) % NX
            part = lax.dot_general(
                value, w_vm[pl.ds(pl.multiple_of(q * 256, 256), 256), :],
                (((1,), (1,)), ((), ())), preferred_element_type=F32,
            )
            if off == half:
                splus[k, 0, 0] = part[:, :128].astype(BF16)
                plus(k, 0).start()
                sminus[k, 0, 1] = part[:, 128:].astype(BF16)
                minus(k, 0).start()
            else:
                pbuf[k, off, 0] = part[:, :128]
                pbuf[k, off, 1] = part[:, 128:]

    def pass_on(k, s):
        plus(k, s - 1).wait_recv()
        for h in range(2):
            value = pbuf[k, half - s, h]
            if s > 1 or h == 0:
                value += rplus[k, s - 1, h].astype(F32)
            splus[k, s, h] = value.astype(BF16)
        plus(k, s).start()
        minus(k, s - 1).wait_recv()
        for h in range(2):
            value = pbuf[k, half + s, h]
            if s > 1 or h == 1:
                value += rminus[k, s - 1, h].astype(F32)
            sminus[k, s, h] = value.astype(BF16)
        minus(k, s).start()

    def collect(k):
        plus(k, half - 1).wait_recv()
        minus(k, half - 1).wait_recv()
        for h in range(2):
            value = pbuf[k, 0, h] + rplus[k, half - 1, h].astype(F32)
            fin[k, h] = value + rminus[k, half - 1, h].astype(F32)
        hsend[k] = fin[k, 1 - yh].astype(BF16)
        swap(k).start()

    def finish(k):
        swap(k).wait_recv()
        fin[k, 0] = fin[k, yh] + hrecv[k].astype(F32)
        at = ((z + NZ - z_step(k)) % NZ) * NC
        for f in range(NC):
            for r in range(NY):
                source = ((y + NY - r) % NY) * (NZ * NC) + at + (c + f) % NC
                start = f * msg + r * cap
                out4[source, 0:cap, :] = fin[k, 0, start:start + cap, :]

    def d_copy(r):
        return remote(
            dsend.at[r - 1], drecv.at[r - 1], d_s.at[r - 1], d_r.at[r - 1],
            dev(y=(y + NY - r) % NY),
        )

    def combine():
        def one(k, carry):
            for f in range(NC):
                m = k * NC + f
                expert = (y * NZ + (z + NZ - z_step(k)) % NZ) * NC + (c + f) % NC
                high, low = pairs(0, expert)
                at = pl.ds(pl.multiple_of(m * msg, 16), msg)
                pa[0, at, :] = high
                pa[1, at, :] = low
            return carry

        lax.fori_loop(0, NZ, one, 0)
        for m in range(1, NZ * NC):
            az_copy(m // NC, m % NC).wait_recv()
        arrived = arecv[...].reshape(total * cap, width)
        over_rows = (((0,), (0,)), ((), ()))
        value = lax.dot_general(
            pa[0], arrived, over_rows, preferred_element_type=F32
        )
        value += lax.dot_general(
            pa[1], arrived, over_rows, preferred_element_type=F32
        )
        for r in range(1, NY):
            dsend[r - 1] = value[r * tok:(r + 1) * tok].astype(BF16)
            d_copy(r).start()
        dense[...] = value[:tok]

    def step(t, carry):
        def at(s, run):
            @pl.when((t >= s) & (t < s + NZ))
            def _():
                run(t - s)

        at(half + 1, finish)
        at(half, collect)
        for s in range(half - 1, 0, -1):
            at(s, functools.partial(pass_on, s=s))
        at(0, product)

        @pl.when(t == SEND_A)
        def _():
            for m in range(1, NZ * NC):
                az_copy(m // NC, m % NC).start()

        @pl.when(t == COMBINE_A)
        def _():
            combine()

        return carry

    lax.fori_loop(0, NZ + half + 2, step, 0)

    for i in range(total):
        gout[i * cap:(i + 1) * cap, :] = out4[i, 0:cap, :]
    grad_ref[...] = gout[...].astype(BF16)

    result = dense[...]
    for r in range(1, NY):
        d_copy(r).wait_recv()
        result += drecv[r - 1].astype(F32)
    mixed_ref[...] = result.astype(BF16)

    for d in range(1, NY):
        y_copy(d).wait_send()
        d_copy(d).wait_send()

    def sent_z(m, carry):
        for f in range(NC):
            if f == 0:
                @pl.when(m > 0)
                def _():
                    bz_copy(m, 0).wait_send()
                    az_copy(m, 0).wait_send()
            else:
                bz_copy(m, f).wait_send()
                az_copy(m, f).wait_send()
        for s in range(half):
            plus(m, s).wait_send()
            minus(m, s).wait_send()
        swap(m).wait_send()
        return carry

    lax.fori_loop(0, NZ, sent_z, 0)


def on_device(hidden_a, expert_weights, routes_a, gates_a, cotangent_b, routes_b, gates_b):
    total = NY * NZ * NC
    _, slots, ff = hidden_a.shape
    cap = slots // total
    tok, width = cotangent_b.shape
    wide = -(-width // 128) * 128
    half, msg, block = NX // 2, NY * cap, NY * cap * NC
    count = NZ * NC
    vm, dma = pltpu.VMEM, pltpu.SemaphoreType.DMA
    whole = pl.BlockSpec(memory_space=pltpu.VMEM)
    anywhere = pl.BlockSpec(memory_space=pl.ANY)
    mixed, grad = pl.pallas_call(
        functools.partial(body, cap),
        out_shape=(
            jax.ShapeDtypeStruct((tok, width), BF16),
            jax.ShapeDtypeStruct((slots, 128), BF16),
        ),
        in_specs=[anywhere, anywhere] + [whole] * 5,
        out_specs=(whole, whole),
        scratch_shapes=[
            vm((slots, ff), BF16),
            vm((ff, width), BF16),
            vm((NY, tok, wide), BF16),
            vm((2, 3, 8, NY * tok), F32),
            vm((total, 16, width), F32),
            vm((msg, width), F32),
            vm((count, msg, width), BF16),
            vm((count, msg, width), BF16),
            vm((count, msg, width), BF16),
            vm((count, msg, width), BF16),
            vm((2, slots, NY * tok), BF16),
            vm((NZ, NX, 2, block, 128), F32),
            vm((NZ, half, 2, block, 128), BF16),
            vm((NZ, half, 2, block, 128), BF16),
            vm((NZ, half, 2, block, 128), BF16),
            vm((NZ, half, 2, block, 128), BF16),
            vm((NZ, 2, block, 128), F32),
            vm((NZ, block, 128), BF16),
            vm((NZ, block, 128), BF16),
            vm((total, 16, 128), F32),
            vm((slots, 128), F32),
            vm((tok, width), F32),
            vm((NY - 1, tok, width), BF16),
            vm((NY - 1, tok, width), BF16),
            dma((2,)),
            dma((NY - 1,)), dma((NY - 1,)),
            dma((count,)), dma((count,)),
            dma((count,)), dma((count,)),
            dma((NZ, half)), dma((NZ, half)),
            dma((NZ, half)), dma((NZ, half)),
            dma((NZ,)), dma((NZ,)),
            dma((NY - 1,)), dma((NY - 1,)),
        ],
        compiler_params=pltpu.CompilerParams(
            collective_id=0, has_side_effects=True,
            vmem_limit_bytes=56 * 1024 * 1024,
        ),
    )(
        hidden_a.reshape(slots, ff), expert_weights.reshape(ff, width),
        routes_a, gates_a, cotangent_b, routes_b, gates_b,
    )
    return mixed, grad.reshape(1, slots, 128)


def solution(mesh):
    in_specs = (
        P("expert", None, None),
        P("expert", None, "pipe"),
        P("expert", None),
        P("expert", None),
        P("expert", "pipe"),
        P("expert", None),
        P("expert", None),
    )
    out_specs = (P("expert", "pipe"), P("expert", None, "pipe"))
    return jax.shard_map(
        on_device, mesh=mesh, in_specs=in_specs, out_specs=out_specs, check_vma=False
    )
```

time: 349 us -> 103 us (0.30)
  the two profiles are of different devices: /device:TPU:1 before, /device:TPU:18 now
where the time goes in v1:
time: 103 us
  Pallas kernels  89.6 us (87%)
  local copies, waits for them, and re-layouts  12.4 us (12%)
    pallas_call x1, Pallas kernels, on_device(): pl.pallas_call(functools.partial(body, cap), out_shape=(jax.ShapeDtypeStr...  89.6 us
    unnamed x7, local copies, waits for them, and re-layouts  12.4 us

profile of v1, /device:TPU:18, one launch (start us, length us, event | category | flops | bytes accessed | tf_op | source)
XLA Modules:
  0.0 102.6 jit_solution(5285821105717706536)
XLA Ops:
  0.6 1.4 %copy.10.ra_ref = s32[64,8]{1,0:T(8,128)} copy(s32[64,8]{0,1:T(8,128)} %param.9) | data formatting | bytes 4096 | tf_op args[2]
  2.0 1.4 %copy.11.ga_ref = f32[64,8]{1,0:T(8,128)} copy(f32[64,8]{0,1:T(8,128)} %param.10) | data formatting | bytes 4096 | tf_op args[3]
  3.4 1.4 %copy.12.rb_ref = s32[64,8]{1,0:T(8,128)} copy(s32[64,8]{0,1:T(8,128)} %param.12) | data formatting | bytes 4096 | tf_op args[5]
  4.8 1.4 %copy.13.gb_ref = f32[64,8]{1,0:T(8,128)} copy(f32[64,8]{0,1:T(8,128)} %param.13) | data formatting | bytes 4096 | tf_op args[6]
  6.1 3.8 %copy.9 = bf16[1,2048,448]{2,1,0:T(8,128)(2,1)} copy(bf16[1,2048,448]{1,2,0:T(8,128)(2,1)} %param.8) | data formatting | bytes 3670016 | tf_op args[1]
  10.0 89.6 %shard_map.86 = (bf16[64,448]{1,0:T(8,128)(2,1)}, bf16[768,128]{1,0:T(8,128)(2,1)}) custom-call(bf16[768,2048]{1,0:T(8,128)(2,1)} %bitcast.4, bf16[2048,448]{1,0:T(8,128)(2,1)} %bitcast.3, s32[64,8]{1,0:T(8,128)} %copy.10.ra_ref, f32[64,8]{1,0:T(8,128)} %copy.11.ga_ref, bf16[64,448]{1,0:T(8,128)(2,1)} %cot_ref.1, s32[64,8]{1,0:T(8,128)} %copy.12.rb_ref, ...), custom_call_target="tpu_custom_call" | custom-call | tf_op jit(solution)/shard_map/pallas_call | solution.py:394
  99.6 1.5 %copy.16 = bf16[64,448]{1,0:T(8,128)(2,1)} copy(bf16[64,448]{1,0:T(8,128)(2,1)} %get-tuple-element.8) | data formatting | bytes 114688
  101.0 1.6 %copy.17 = bf16[1,768,128]{2,1,0:T(8,128)(2,1)} copy(bf16[1,768,128]{2,1,0:T(8,128)(2,1)} %bitcast.5) | data formatting | bytes 393216

commit v2 on v1

--- a/solution.py
+++ b/solution.py
@@ -9,7 +9,8 @@
 
 NX, NYH = 8, 2
 NY, NZ, NC = 4, 8, 2
-SEND_A, COMBINE_A = 1, 9
+SEND_A, COMBINE_A = 4, 13
+LAG, SWAP_LAG = 2, 3
 
 BF16, F32 = jnp.bfloat16, jnp.float32
 
@@ -25,7 +26,7 @@
     h_s, h_r, d_s, d_r,
 ):
     tok, width = cot_ref.shape
-    top = ra_ref.shape[1]
+    top = ra_ref.shape[0]
     total = NY * NZ * NC
     msg = NY * cap
     half = NX // 2
@@ -66,38 +67,41 @@
             barrier, inc=1, device_id=to, device_id_type=pl.DeviceIdType.MESH
         )
 
-    lane = lax.broadcasted_iota(jnp.int32, (tok, 128), 1)
     base = width - (wide - 128)
+
+    def mask(test, shape):
+        rows = lax.broadcasted_iota(jnp.int32, shape, 0)
+        cols = lax.broadcasted_iota(jnp.int32, shape, 1)
+        return test(rows, cols).astype(F32).astype(BF16)
+
+    after = mask(lambda i, j: i < j, (tok, tok))
+    expert_row = lax.broadcasted_iota(jnp.int32, (total, tok), 0)
+    notes = []
+    for r_ref, g_ref in ((ra_ref, ga_ref), (rb_ref, gb_ref)):
+        routes = r_ref[...]
+        gates = g_ref[...]
+        high = gates.astype(BF16)
+        low = (gates - high.astype(F32)).astype(BF16)
+        hit = [routes[k:k + 1, :] == expert_row for k in range(top)]
+        member = jnp.zeros((total, tok), F32)
+        for k in range(top):
+            member = jnp.where(hit[k], 1.0, member)
+        rank = jnp.dot(member.astype(BF16), after, preferred_element_type=F32)
+        slot = [
+            jnp.sum(jnp.where(hit[k], rank, 0.0), axis=0, keepdims=True)
+            for k in range(top)
+        ]
+        notes += [routes.astype(F32), jnp.concatenate(slot, axis=0)]
+        notes += [high.astype(F32), low.astype(F32)]
     tail = jnp.dot(
-        cot_ref[:, wide - 128:],
-        (
-            lax.broadcasted_iota(jnp.int32, (base, 128), 0)
-            == lax.broadcasted_iota(jnp.int32, (base, 128), 1)
-        ).astype(F32).astype(BF16),
+        cot_ref[:, wide - 128:], mask(lambda i, j: i == j, (base, 128)),
         preferred_element_type=F32,
     )
-    before = (
-        lax.broadcasted_iota(jnp.int32, (tok, tok), 0)
-        > lax.broadcasted_iota(jnp.int32, (tok, tok), 1)
-    ).astype(F32).astype(BF16)
-    for n, (r_ref, g_ref) in enumerate(((ra_ref, ga_ref), (rb_ref, gb_ref))):
-        first = base + n * 4 * 8
-        routes = r_ref[...]
-        gates = g_ref[...]
-        high = gates.astype(BF16).astype(F32)
-        low = (gates - high).astype(BF16).astype(F32)
-        names = routes.astype(F32)
-        hit = [routes[:, k:k + 1] == lane for k in range(top)]
-        member = jnp.zeros((tok, 128), F32)
-        for k in range(top):
-            member = jnp.where(hit[k], 1.0, member)
-        rank = jnp.dot(before, member.astype(BF16), preferred_element_type=F32)
-        for k in range(top):
-            slot = jnp.sum(jnp.where(hit[k], rank, 0.0), axis=1, keepdims=True)
-            tail = jnp.where(lane == first + k, names[:, k:k + 1], tail)
-            tail = jnp.where(lane == first + 8 + k, slot, tail)
-            tail = jnp.where(lane == first + 16 + k, high[:, k:k + 1], tail)
-            tail = jnp.where(lane == first + 24 + k, low[:, k:k + 1], tail)
+    tail += jnp.dot(
+        jnp.concatenate(notes, axis=0).astype(BF16),
+        mask(lambda i, j: i + base == j, (tok, 128)),
+        preferred_element_type=F32,
+    )
     gath[0, :, :wide - 128] = cot_ref[:, :wide - 128]
     gath[0, :, wide - 128:] = tail.astype(BF16)
 
@@ -118,9 +122,9 @@
     rows = NZ * NC * cap
 
     def forward(j, carry):
-        value = jnp.dot(
+        value = lax.dot_general(
             h_vm[pl.ds(pl.multiple_of(j * rows, 16), rows), :], w_vm[...],
-            preferred_element_type=F32,
+            (((1,), (1,)), ((), ())), preferred_element_type=F32,
         )
         for i in range(NZ * NC):
             fwd[j * (NZ * NC) + i, 0:cap, :] = value[i * cap:(i + 1) * cap, :]
@@ -143,16 +147,17 @@
     for d in range(1, NY):
         y_copy(d).wait_recv()
 
-    for n in range(2):
-        for r in range(NY):
-            info = gath[r, :, wide - 128:].astype(F32).T
-            first = base + n * 4 * 8
-            cols = slice(r * tok, (r + 1) * tok)
-            codes[n, 0, :, cols] = (
-                info[first:first + 8] * 16.0 + info[first + 8:first + 16]
-            )
-            codes[n, 1, :, cols] = info[first + 16:first + 24]
-            codes[n, 2, :, cols] = info[first + 24:first + 32]
+    for r in range(0, NY, 2):
+        left = pltpu.roll(gath[r, :, wide - 128:].astype(F32), 128 - base, 1)
+        right = gath[r + 1, :, wide - 128:].astype(F32)
+        lane = lax.broadcasted_iota(jnp.int32, (tok, 128), 1)
+        info = jnp.where(lane < tok, left, right)
+        cols = slice(r * tok, (r + 2) * tok)
+        for n in range(2):
+            at = n * 4 * 8
+            codes[n, 0, :, cols] = info[at:at + 8] * 16.0 + info[at + 8:at + 16]
+            codes[n, 1, :, cols] = info[at + 16:at + 24]
+            codes[n, 2, :, cols] = info[at + 24:at + 32]
 
     row = lax.broadcasted_iota(jnp.int32, (msg, NY * tok), 0)
     col = lax.broadcasted_iota(jnp.int32, (msg, NY * tok), 1)
@@ -192,13 +197,15 @@
         expert = (y * NZ + (z + z_step(k)) % NZ) * NC + (c + f) % NC
         high, low = pairs(1, expert)
         cots = gath[...].reshape(NY * tok, wide)
-        value = jnp.dot(high, cots, preferred_element_type=F32)
-        value += jnp.dot(low, cots, preferred_element_type=F32)
-        return value[:, :width].astype(BF16)
+        value = jnp.dot(
+            jnp.concatenate([high, low], axis=0), cots, preferred_element_type=F32
+        )
+        return (value[:msg, :width] + value[msg:, :width]).astype(BF16)
 
     for f in range(1, NC):
         bsend[f] = fill(0, f)
         bz_copy(0, f).start()
+    brecv[0] = fill(0, 0)
 
     def fill_step(k, carry):
         for f in range(NC):
@@ -206,10 +213,8 @@
             bz_copy(k, f).start()
         return carry
 
-    lax.fori_loop(1, NZ, fill_step, 0)
-    brecv[0] = fill(0, 0)
-
     block = NC * msg
+    blocks = NZ
 
     def plus(k, s):
         to, sems = dev(x=(x + 1) % NX), (xp_s.at[k, s], xp_r.at[k, s])
@@ -229,21 +234,21 @@
         )
 
     def product(k):
-        @pl.when(k > 0)
-        def _():
-            bz_copy(k, 0).wait_recv()
-
-        for f in range(1, NC):
-            bz_copy(k, f).wait_recv()
+        if isinstance(k, int):
+            for f in range(1, NC):
+                bz_copy(k, f).wait_recv()
+        else:
+            for f in range(NC):
+                bz_copy(k, f).wait_recv()
         value = brecv[pl.ds(k * NC, NC)].reshape(block, width)
         order = [half]
         for i in range(half - 1, 0, -1):
             order += [i, NX - i]
         for off in order + [0]:
             q = (x + off) % NX
-            part = lax.dot_general(
-                value, w_vm[pl.ds(pl.multiple_of(q * 256, 256), 256), :],
-                (((1,), (1,)), ((), ())), preferred_element_type=F32,
+            part = jnp.dot(
+                value, w_vm[:, pl.ds(pl.multiple_of(q * 256, 256), 256)],
+                preferred_element_type=F32,
             )
             if off == half:
                 splus[k, 0, 0] = part[:, :128].astype(BF16)
@@ -324,15 +329,18 @@
 
     def step(t, carry):
         def at(s, run):
-            @pl.when((t >= s) & (t < s + NZ))
+            @pl.when((t >= s) & (t < s + blocks))
             def _():
                 run(t - s)
 
-        at(half + 1, finish)
-        at(half, collect)
+        at(half * LAG + SWAP_LAG, finish)
+        at(half * LAG, collect)
         for s in range(half - 1, 0, -1):
-            at(s, functools.partial(pass_on, s=s))
-        at(0, product)
+            at(s * LAG, functools.partial(pass_on, s=s))
+
+        @pl.when((t > 0) & (t < blocks))
+        def _():
+            product(t)
 
         @pl.when(t == SEND_A)
         def _():
@@ -345,7 +353,10 @@
 
         return carry
 
-    lax.fori_loop(0, NZ + half + 2, step, 0)
+    lax.fori_loop(1, 3, fill_step, 0)
+    product(0)
+    lax.fori_loop(3, NZ, fill_step, 0)
+    lax.fori_loop(0, blocks + half * LAG + SWAP_LAG, step, 0)
 
     for i in range(total):
         gout[i * cap:(i + 1) * cap, :] = out4[i, 0:cap, :]
@@ -401,7 +412,7 @@
         out_specs=(whole, whole),
         scratch_shapes=[
             vm((slots, ff), BF16),
-            vm((ff, width), BF16),
+            vm((width, ff), BF16),
             vm((NY, tok, wide), BF16),
             vm((2, 3, 8, NY * tok), F32),
             vm((total, 16, width), F32),
@@ -438,8 +449,8 @@
             vmem_limit_bytes=56 * 1024 * 1024,
         ),
     )(
-        hidden_a.reshape(slots, ff), expert_weights.reshape(ff, width),
-        routes_a, gates_a, cotangent_b, routes_b, gates_b,
+        hidden_a.reshape(slots, ff), expert_weights.reshape(ff, width).T,
+        routes_a.T, gates_a.T, cotangent_b, routes_b.T, gates_b.T,
     )
     return mixed, grad.reshape(1, slots, 128)
 

time: 103 us -> 87.4 us (0.85)
  the two profiles are of different devices: /device:TPU:18 before, /device:TPU:1 now
where the time goes in v2:
time: 87.4 us; the launch traced here: 87.1 us
  Pallas kernels  83.4 us (95%)
  local copies, waits for them, and re-layouts  3.09 us (4%)
    pallas_call x1, Pallas kernels, on_device(): pl.pallas_call(functools.partial(body, cap), out_shape=(jax.ShapeDtypeStr...  83.4 us
    unnamed x2, local copies, waits for them, and re-layouts  3.09 us

profile of v2, /device:TPU:1, one launch (start us, length us, event | category | flops | bytes accessed | tf_op | source)
XLA Modules:
  0.0 87.1 jit_solution(9103058610793247624)
XLA Ops:
  0.6 83.4 %shard_map.86 = (bf16[64,448]{1,0:T(8,128)(2,1)}, bf16[768,128]{1,0:T(8,128)(2,1)}) custom-call(bf16[768,2048]{1,0:T(8,128)(2,1)} %bitcast.9, bf16[448,2048]{1,0:T(8,128)(2,1)} %bitcast.10, s32[8,64]{1,0:T(8,128)} %bitcast.12, f32[8,64]{1,0:T(8,128)} %bitcast.13, bf16[64,448]{1,0:T(8,128)(2,1)} %cot_ref.1, s32[8,64]{1,0:T(8,128)} %bitcast.14, f32[8,64]{1,0:T(8,128)} %bitcast.15), custom_call_target="tpu_custom_call" | custom-call | tf_op jit(solution)/shard_map/pallas_call | solution.py:405
  84.0 1.5 %copy.11 = bf16[64,448]{1,0:T(8,128)(2,1)} copy(bf16[64,448]{1,0:T(8,128)(2,1)} %get-tuple-element.8) | data formatting | bytes 114688
  85.5 1.6 %copy.12 = bf16[1,768,128]{2,1,0:T(8,128)(2,1)} copy(bf16[1,768,128]{2,1,0:T(8,128)(2,1)} %bitcast.11) | data formatting | bytes 393216

commit v3 on v2

--- a/solution.py
+++ b/solution.py
@@ -9,7 +9,8 @@
 
 NX, NYH = 8, 2
 NY, NZ, NC = 4, 8, 2
-SEND_A, COMBINE_A = 4, 13
+EARLY_A, SEND_A, COMBINE_A = 7, 2, 10
+TRADE = 2
 LAG, SWAP_LAG = 2, 3
 
 BF16, F32 = jnp.bfloat16, jnp.float32
@@ -17,13 +18,13 @@
 
 def body(
     cap,
-    h_hbm, w_hbm, ra_ref, ga_ref, cot_ref, rb_ref, gb_ref,
+    h_hbm, w_hbm, ra_hbm, ga_hbm, cot_hbm, rb_hbm, gb_hbm,
     mixed_ref, grad_ref,
-    h_vm, w_vm, gath, codes, fwd, tile48, asend, arecv, bsend, brecv, pa,
+    ra_ref, ga_ref, cot_ref, rb_ref, gb_ref, h_vm, w_vm, gath, codes, fwd, tile48, asend, arecv, bsend, brecv, pa,
     pbuf, splus, sminus, rplus, rminus, fin, hsend, hrecv, out4, gout,
-    dense, dsend, drecv,
+    dense, dsend, drecv, both, tsend, trecv,
     load_sem, y_s, y_r, az_s, az_r, bz_s, bz_r, xp_s, xp_r, xm_s, xm_r,
-    h_s, h_r, d_s, d_r,
+    h_s, h_r, d_s, d_r, t_s, t_r,
 ):
     tok, width = cot_ref.shape
     top = ra_ref.shape[0]
@@ -52,9 +53,6 @@
 
     load_w = pltpu.make_async_copy(w_hbm, w_vm, load_sem.at[0])
     load_h = pltpu.make_async_copy(h_hbm, h_vm, load_sem.at[1])
-    load_w.start()
-    load_h.start()
-
     partners = [dev(y=(y + d) % NY) for d in range(1, NY)]
     partners += [
         dev(z=(z + d) % NZ, c=(c + f) % NC)
@@ -66,6 +64,19 @@
         pl.semaphore_signal(
             barrier, inc=1, device_id=to, device_id_type=pl.DeviceIdType.MESH
         )
+    small = [
+        pltpu.make_async_copy(src, dst, load_sem.at[2 + n])
+        for n, (src, dst) in enumerate((
+            (ra_hbm, ra_ref), (ga_hbm, ga_ref), (rb_hbm, rb_ref),
+            (gb_hbm, gb_ref), (cot_hbm, cot_ref),
+        ))
+    ]
+    for copy in small:
+        copy.start()
+    load_w.start()
+    load_h.start()
+    for copy in small:
+        copy.wait()
 
     base = width - (wide - 128)
 
@@ -144,6 +155,23 @@
     lax.fori_loop(0, NZ, pack_a, 0)
     arecv[0] = asend[0]
 
+    def az_copy(k, f):
+        m = k * NC + f
+        return remote(
+            asend.at[m], arecv.at[m], az_s.at[m], az_r.at[m],
+            dev(z=(z + z_step(k)) % NZ, c=(c + f) % NC),
+        )
+
+    def send_a(first, last):
+        def one(k, carry):
+            for f in range(NC):
+                az_copy(k, f).start()
+            return carry
+
+        lax.fori_loop(first, last, one, 0)
+
+    send_a(EARLY_A, NZ)
+
     for d in range(1, NY):
         y_copy(d).wait_recv()
 
@@ -186,13 +214,6 @@
             dev(z=(z + z_step(k)) % NZ, c=(c + f) % NC),
         )
 
-    def az_copy(k, f):
-        m = k * NC + f
-        return remote(
-            asend.at[m], arecv.at[m], az_s.at[m], az_r.at[m],
-            dev(z=(z + z_step(k)) % NZ, c=(c + f) % NC),
-        )
-
     def fill(k, f):
         expert = (y * NZ + (z + z_step(k)) % NZ) * NC + (c + f) % NC
         high, low = pairs(1, expert)
@@ -232,6 +253,77 @@
         return remote(
             hsend.at[k], hrecv.at[k], h_s.at[k], h_r.at[k], dev(yh=1 - yh)
         )
+
+    def trade():
+        return remote(tsend, trecv, t_s, t_r, dev(yh=1 - yh))
+
+    def at_step(p):
+        return lax.select(p == 0, 0, lax.select(p == blocks - 1, 1, p + 1))
+
+    def traded_product():
+        for f in range(NC):
+            bz_copy(1, f).wait_recv()
+        value = brecv[NC:2 * NC].reshape(block, width)
+        for off in range(NX):
+            q = (x + off) % NX
+            part = jnp.dot(
+                value, w_vm[:, pl.ds(pl.multiple_of(q * 256, 256), 256)],
+                preferred_element_type=F32,
+            )
+            both[0] = part[:, :128]
+            both[1] = part[:, 128:]
+            tsend[off] = both[1 - yh].astype(BF16)
+            pbuf[1, off, 0] = both[yh]
+        trade().start()
+
+    def traded_plus(s):
+        return remote(
+            splus.at[1, s, 0], rplus.at[1, s, 0], xp_s.at[1, s], xp_r.at[1, s],
+            dev(x=(x + 1) % NX),
+        )
+
+    def traded_minus(s):
+        return remote(
+            sminus.at[1, s, 0], rminus.at[1, s, 0], xm_s.at[1, s], xm_r.at[1, s],
+            dev(x=(x + NX - 1) % NX),
+        )
+
+    def traded_first():
+        trade().wait_recv()
+        for off in [half] + [i for i in range(NX) if i != half]:
+            value = pbuf[1, off, 0] + trecv[off].astype(F32)
+            if off == half:
+                splus[1, 0, 0] = value.astype(BF16)
+                traded_plus(0).start()
+            else:
+                pbuf[1, off, 0] = value
+
+    def traded_pass(s):
+        traded_plus(s - 1).wait_recv()
+        value = pbuf[1, half - s, 0] + rplus[1, s - 1, 0].astype(F32)
+        splus[1, s, 0] = value.astype(BF16)
+        traded_plus(s).start()
+        value = pbuf[1, half + s, 0]
+        if s > 1:
+            traded_minus(s - 1).wait_recv()
+            value += rminus[1, s - 1, 0].astype(F32)
+        sminus[1, s, 0] = value.astype(BF16)
+        traded_minus(s).start()
+
+    def scatter(k):
+        at = ((z + NZ - z_step(k)) % NZ) * NC
+        for f in range(NC):
+            for r in range(NY):
+                source = ((y + NY - r) % NY) * (NZ * NC) + at + (c + f) % NC
+                start = f * msg + r * cap
+                out4[source, 0:cap, :] = fin[k, 0, start:start + cap, :]
+
+    def traded_collect():
+        traded_plus(half - 1).wait_recv()
+        traded_minus(half - 1).wait_recv()
+        value = pbuf[1, 0, 0] + rplus[1, half - 1, 0].astype(F32)
+        fin[1, 0] = value + rminus[1, half - 1, 0].astype(F32)
+        scatter(1)
 
     def product(k):
         if isinstance(k, int):
@@ -287,12 +379,7 @@
     def finish(k):
         swap(k).wait_recv()
         fin[k, 0] = fin[k, yh] + hrecv[k].astype(F32)
-        at = ((z + NZ - z_step(k)) % NZ) * NC
-        for f in range(NC):
-            for r in range(NY):
-                source = ((y + NY - r) % NY) * (NZ * NC) + at + (c + f) % NC
-                start = f * msg + r * cap
-                out4[source, 0:cap, :] = fin[k, 0, start:start + cap, :]
+        scatter(k)
 
     def d_copy(r):
         return remote(
@@ -300,18 +387,16 @@
             dev(y=(y + NY - r) % NY),
         )
 
+    def rows_a(k):
+        for f in range(NC):
+            m = k * NC + f
+            expert = (y * NZ + (z + NZ - z_step(k)) % NZ) * NC + (c + f) % NC
+            high, low = pairs(0, expert)
+            at = pl.ds(pl.multiple_of(m * msg, 16), msg)
+            pa[0, at, :] = high
+            pa[1, at, :] = low
+
     def combine():
-        def one(k, carry):
-            for f in range(NC):
-                m = k * NC + f
-                expert = (y * NZ + (z + NZ - z_step(k)) % NZ) * NC + (c + f) % NC
-                high, low = pairs(0, expert)
-                at = pl.ds(pl.multiple_of(m * msg, 16), msg)
-                pa[0, at, :] = high
-                pa[1, at, :] = low
-            return carry
-
-        lax.fori_loop(0, NZ, one, 0)
         for m in range(1, NZ * NC):
             az_copy(m // NC, m % NC).wait_recv()
         arrived = arecv[...].reshape(total * cap, width)
@@ -329,23 +414,41 @@
 
     def step(t, carry):
         def at(s, run):
-            @pl.when((t >= s) & (t < s + blocks))
+            @pl.when((t >= s) & (t < s + blocks - 1))
             def _():
-                run(t - s)
+                run(at_step(t - s))
+
+        def last(s, run):
+            @pl.when(t == s + blocks - 1)
+            def _():
+                run()
 
         at(half * LAG + SWAP_LAG, finish)
         at(half * LAG, collect)
+        last(half * LAG, traded_collect)
         for s in range(half - 1, 0, -1):
             at(s * LAG, functools.partial(pass_on, s=s))
-
-        @pl.when((t > 0) & (t < blocks))
+            last(s * LAG, functools.partial(traded_pass, s))
+
+        last(0, traded_first)
+
+        @pl.when((t > 0) & (t < blocks - 1))
         def _():
-            product(t)
+            product(at_step(t))
+
+        @pl.when(t == TRADE)
+        def _():
+            traded_product()
+
+        @pl.when((t >= 1) & (t <= NZ))
+        def _():
+            rows_a(t - 1)
 
         @pl.when(t == SEND_A)
         def _():
-            for m in range(1, NZ * NC):
-                az_copy(m // NC, m % NC).start()
+            for f in range(1, NC):
+                az_copy(0, f).start()
+            send_a(1, EARLY_A)
 
         @pl.when(t == COMBINE_A)
         def _():
@@ -382,13 +485,26 @@
             else:
                 bz_copy(m, f).wait_send()
                 az_copy(m, f).wait_send()
-        for s in range(half):
-            plus(m, s).wait_send()
-            minus(m, s).wait_send()
-        swap(m).wait_send()
+        @pl.when(m != 1)
+        def _():
+            for s in range(half):
+                plus(m, s).wait_send()
+                minus(m, s).wait_send()
+            swap(m).wait_send()
+
         return carry
 
     lax.fori_loop(0, NZ, sent_z, 0)
+    trade().wait_send()
+    for s in range(half):
+        traded_plus(s).wait_send()
+        if s:
+            traded_minus(s).wait_send()
+
+
+def write(mixed_in, grad_in, mixed_out, grad_out):
+    mixed_out[...] = mixed_in[...]
+    grad_out[...] = grad_in[...]
 
 
 def on_device(hidden_a, expert_weights, routes_a, gates_a, cotangent_b, routes_b, gates_b):
@@ -408,9 +524,14 @@
             jax.ShapeDtypeStruct((tok, width), BF16),
             jax.ShapeDtypeStruct((slots, 128), BF16),
         ),
-        in_specs=[anywhere, anywhere] + [whole] * 5,
+        in_specs=[anywhere] * 7,
         out_specs=(whole, whole),
         scratch_shapes=[
+            vm(routes_a.T.shape, routes_a.dtype),
+            vm(gates_a.T.shape, F32),
+            vm((tok, width), BF16),
+            vm(routes_b.T.shape, routes_b.dtype),
+            vm(gates_b.T.shape, F32),
             vm((slots, ff), BF16),
             vm((width, ff), BF16),
             vm((NY, tok, wide), BF16),
@@ -435,14 +556,17 @@
             vm((tok, width), F32),
             vm((NY - 1, tok, width), BF16),
             vm((NY - 1, tok, width), BF16),
-            dma((2,)),
+            vm((2, block, 128), F32),
+            vm((NX, block, 128), BF16),
+            vm((NX, block, 128), BF16),
+            dma((7,)),
             dma((NY - 1,)), dma((NY - 1,)),
             dma((count,)), dma((count,)),
             dma((count,)), dma((count,)),
             dma((NZ, half)), dma((NZ, half)),
             dma((NZ, half)), dma((NZ, half)),
             dma((NZ,)), dma((NZ,)),
-            dma((NY - 1,)), dma((NY - 1,)),
+            dma((NY - 1,)), dma((NY - 1,)), dma, dma,
         ],
         compiler_params=pltpu.CompilerParams(
             collective_id=0, has_side_effects=True,
@@ -452,6 +576,15 @@
         hidden_a.reshape(slots, ff), expert_weights.reshape(ff, width).T,
         routes_a.T, gates_a.T, cotangent_b, routes_b.T, gates_b.T,
     )
+    mixed, grad = pl.pallas_call(
+        write,
+        out_shape=(
+            jax.ShapeDtypeStruct((tok, width), BF16),
+            jax.ShapeDtypeStruct((slots, 128), BF16),
+        ),
+        in_specs=[whole, whole],
+        out_specs=(whole, whole),
+    )(mixed, grad)
     return mixed, grad.reshape(1, slots, 128)
 
 

time: 87.4 us -> 83.2 us (0.952)
  local copies, waits for them, and re-layouts: 3.09 us -> 0 us
  Pallas kernels: 83.4 us -> 81.9 us
    pallas_call x1, Pallas kernels: 83.4 us -> 80.2 us  [on_device(): pl.pallas_call(functools.partial(body, cap), out_shape=(jax.ShapeDtypeStr...]
    unnamed x2 -> x0, local copies, waits for them, and re-layouts: 3.09 us -> none
    pallas_call x0 -> x1, Pallas kernels: none -> 1.67 us  [on_device(): pl.pallas_call(write, out_shape=(jax.ShapeDtypeStruct((tok, width), BF16)...]
where the time goes in v3:
time: 83.2 us; the launch traced here: 82.5 us
  Pallas kernels  81.9 us (98%)
    pallas_call x1, Pallas kernels, on_device(): pl.pallas_call(functools.partial(body, cap), out_shape=(jax.ShapeDtypeStr...  80.2 us
    pallas_call x1, Pallas kernels, on_device(): pl.pallas_call(write, out_shape=(jax.ShapeDtypeStruct((tok, width), BF16)...  1.67 us

profile of v3, /device:TPU:1, one launch (start us, length us, event | category | flops | bytes accessed | tf_op | source)
XLA Modules:
  0.0 82.5 jit_solution(3669075995669556044)
XLA Ops:
  0.6 80.2 %shard_map.86 = (bf16[64,448]{1,0:T(8,128)(2,1)}, bf16[768,128]{1,0:T(8,128)(2,1)}) custom-call(bf16[768,2048]{1,0:T(8,128)(2,1)} %bitcast.9, bf16[448,2048]{1,0:T(8,128)(2,1)} %bitcast.10, s32[8,64]{1,0:T(8,128)} %bitcast.11, f32[8,64]{1,0:T(8,128)} %bitcast.12, bf16[64,448]{1,0:T(8,128)(2,1)} %cot_hbm.1, s32[8,64]{1,0:T(8,128)} %bitcast.13, f32[8,64]{1,0:T(8,128)} %bitcast.14), custom_call_target="tpu_custom_call" | custom-call | tf_op jit(solution)/shard_map/pallas_call | solution.py:521
  80.9 1.7 %shard_map.87 = (bf16[64,448]{1,0:T(8,128)(2,1)}, bf16[768,128]{1,0:T(8,128)(2,1)}) custom-call(bf16[64,448]{1,0:T(8,128)(2,1)} %get-tuple-element.6.mixed_in, bf16[768,128]{1,0:T(8,128)(2,1)} %get-tuple-element.7.grad_in), custom_call_target="tpu_custom_call" | custom-call | tf_op jit(solution)/shard_map/pallas_call | solution.py:579

commit v4 on v3

--- a/solution.py
+++ b/solution.py
@@ -9,7 +9,7 @@
 
 NX, NYH = 8, 2
 NY, NZ, NC = 4, 8, 2
-EARLY_A, SEND_A, COMBINE_A = 7, 2, 10
+EARLY_A, SEND_A, COMBINE_A = 7, 1, 9
 TRADE = 2
 LAG, SWAP_LAG = 2, 3
 

time: 83.2 us -> 82.7 us (level)
  no operation moved by 1% of the time
where the time goes in v4:
time: 82.7 us; the launch traced here: 82.5 us
  Pallas kernels  81.9 us (99%)
    pallas_call x1, Pallas kernels, on_device(): pl.pallas_call(functools.partial(body, cap), out_shape=(jax.ShapeDtypeStr...  80.2 us
    pallas_call x1, Pallas kernels, on_device(): pl.pallas_call(write, out_shape=(jax.ShapeDtypeStruct((tok, width), BF16)...  1.67 us

profile of v4, /device:TPU:1, one launch (start us, length us, event | category | flops | bytes accessed | tf_op | source)
XLA Modules:
  0.0 82.5 jit_solution(7172462328300644102)
XLA Ops:
  0.6 80.2 %shard_map.86 = (bf16[64,448]{1,0:T(8,128)(2,1)}, bf16[768,128]{1,0:T(8,128)(2,1)}) custom-call(bf16[768,2048]{1,0:T(8,128)(2,1)} %bitcast.9, bf16[448,2048]{1,0:T(8,128)(2,1)} %bitcast.10, s32[8,64]{1,0:T(8,128)} %bitcast.11, f32[8,64]{1,0:T(8,128)} %bitcast.12, bf16[64,448]{1,0:T(8,128)(2,1)} %cot_hbm.1, s32[8,64]{1,0:T(8,128)} %bitcast.13, f32[8,64]{1,0:T(8,128)} %bitcast.14), custom_call_target="tpu_custom_call" | custom-call | tf_op jit(solution)/shard_map/pallas_call | solution.py:521
  80.9 1.7 %shard_map.87 = (bf16[64,448]{1,0:T(8,128)(2,1)}, bf16[768,128]{1,0:T(8,128)(2,1)}) custom-call(bf16[64,448]{1,0:T(8,128)(2,1)} %get-tuple-element.6.mixed_in, bf16[768,128]{1,0:T(8,128)(2,1)} %get-tuple-element.7.grad_in), custom_call_target="tpu_custom_call" | custom-call | tf_op jit(solution)/shard_map/pallas_call | solution.py:579
